TPU v7x, 512 devices: a whole 4x4x16 slice. The times are simulated.
512 devices in a mesh: blk: 16 (over x, y_lo, core), rep: 32 (over z, y_hi).
Axes of the slice: x: 4, y: 4 (y_hi: 2, y_lo: 2; y = y_hi * 2 + y_lo), z: 16, core: 2. Of those that a mesh axis runs over, the one named last changes fastest.
Arguments:
- features: bfloat16 [65536, 256], P(('blk', 'rep')), may hold values from -6 to 6
- weight_one: bfloat16 [256, 256], replicated, may hold values from -0.375 to 0.375
- weight_two: bfloat16 [256, 256], replicated, may hold values from -0.375 to 0.375
- tile_values: bfloat16 [16, 32, 24, 128, 128], P('blk', 'rep'), may hold values from -0.125 to 0.125
- tile_rows: int32 [16, 32, 24], P('blk', 'rep'), may hold values from 0 to 31, as said below
- tile_cols: int32 [16, 32, 24], P('blk', 'rep'), may hold values from 0 to 511, as said below
- tile_count: int32 [16, 32], P('blk', 'rep'), may hold values from 16 to 24, as said below
Outputs:
- aggregated: bfloat16 [65536, 256], P(('blk', 'rep'))
Inputs may be any that keep to these rules, and one draw needn't show every extreme that they name: `tile_rows`: block row within the holder's row group into which a tile adds; slots k >= tile_count are ignored. `tile_cols`: A tile held at rep index r has column block j * 32 + r for some j: its columns are nodes held by a device of rep index r. `tile_count`: one device holds exactly 24 live tiles.
All inputs are finite; a program needn't handle non-finite values.
Results may differ from a plain program's by a relative error of at most 0.035.
Values may be sent and summed in bfloat16 or wider, within the bound.
A program may use at most 64 MiB of HBM per device.

v0:
```python
import jax
import jax.numpy as jnp
from jax import lax
from jax.sharding import PartitionSpec as P


def tile_products(panel_rows, tile_vals, local_block, block_size, feat_width):
    gathered = lax.all_gather(panel_rows, "blk", axis=0, tiled=True)
    source = gathered.reshape(-1, block_size, feat_width)[local_block]
    return jnp.einsum("kab,kbf->kaf", tile_vals, source, preferred_element_type=jnp.float32)


def body(features, weight_one, weight_two, tile_values, tile_rows, tile_cols, tile_count):
    tile_vals = tile_values[0, 0]
    tile_row = tile_rows[0, 0]
    tile_col = tile_cols[0, 0]
    live_count = tile_count[0, 0]
    feat_width = features.shape[1]
    block_size = tile_vals.shape[-1]
    rows_dev = features.shape[0]
    sub_blocks = rows_dev // block_size
    replicas = lax.axis_size("rep")
    group_blocks = sub_blocks * replicas
    tile_slots = tile_vals.shape[0]
    local_block = tile_col // (replicas * sub_blocks) * sub_blocks + tile_col % sub_blocks
    is_live = (lax.iota(jnp.int32, tile_slots) < live_count).astype(jnp.float32)
    hidden = features
    result = features
    for layer_id in range(2):
        weight = weight_one if layer_id == 0 else weight_two
        panel_rows = jnp.dot(hidden, weight, preferred_element_type=jnp.float32).astype(
            jnp.bfloat16
        )
        products = tile_products(panel_rows, tile_vals, local_block, block_size, feat_width)
        masked = products * is_live[:, None, None]
        partial_value = jax.ops.segment_sum(masked, tile_row, num_segments=group_blocks)
        partial_value = partial_value.astype(jnp.bfloat16).astype(jnp.float32)
        partial_value = partial_value.reshape(group_blocks * block_size, feat_width)
        group_sum = lax.psum(partial_value.astype(jnp.bfloat16), "rep").astype(jnp.float32)
        row_start = lax.axis_index("rep") * rows_dev
        summed = lax.dynamic_slice_in_dim(group_sum, row_start, rows_dev, 0)
        if layer_id == 0:
            hidden = jnp.maximum(summed, 0.0).astype(jnp.bfloat16)
        else:
            result = summed.astype(jnp.bfloat16)
    return result


def solution(mesh):
    in_specs = (
        P(("blk", "rep"), None),
        P(),
        P(),
        P("blk", "rep", None, None, None),
        P("blk", "rep", None),
        P("blk", "rep", None),
        P("blk", "rep"),
    )
    out_specs = P(("blk", "rep"), None)
    return jax.shard_map(body, mesh=mesh, in_specs=in_specs, out_specs=out_specs, check_vma=False)
```

profile of v0, /device:TPU:6, one launch (start us, length us, event | category | flops | bytes accessed | tf_op | source)
XLA Modules:
  0.0 777.0 jit_solution(7862365990700704405)
XLA Ops:
  6.5 0.0 copy-start
  6.5 0.0 all-gather.3.cloned.1.call-start
  6.5 1.8 convolution_convert_fusion.1
  8.3 0.0 all-gather.3.cloned.1.call-update
  8.4 0.0 all-reduce.3.cloned.1.call-start
  9.1 0.7 fusion.4
  9.8 43.4 %all-gather.3.cloned.1.call-done = bf16[2048,256]{1,0:T(8,128)(2,1)} async-done(((bf16[128,256]{1,0:T(8,128)(2,1)}), bf16[2048,256]{1,0:T(8,128)(2,1)}) %all-gather.3.cloned.1.call-update) | async-done | bytes 1048592 | tf_op jit(solution)/shard_map/all_gather | solution.py:8
  53.1 1.9 gather_fusion
  55.0 0.0 copy-done
  55.0 2.4 multiply_bitcast_fusion.1
  57.4 3.6 copy.11
  60.9 0.0 copy-start.2
  60.9 2.4 broadcast.95.clone
  63.4 0.0 copy-done.2
  63.4 9.5 %scatter_fusion = f32[32,128,256]{2,1,0:T(8,128)} fusion(f32[32,128,256]{2,1,0:T(8,128)} %broadcast.95.clone, s32[24]{0:T(128)S(1)} %bitcast.37, f32[24,128,256]{2,1,0:T(8,128)} %copy.11), kind=kCustom, calls=%fused_computation.2 | custom fusion | flops 786432 | bytes 9437280 | tf_op jit(solution)/shard_map/scatter-add | solution.py:36
  72.9 0.0 copy-start.1
  72.9 3.8 convert_element_type.43
  76.7 0.0 all-reduce.3.cloned.1.call-update
  76.7 0.0 all-gather.5.cloned.1.call-start
  76.8 315.6 %all-reduce.3.cloned.1.call-done = bf16[4096,256]{1,0:T(8,128)(2,1)} async-done(((bf16[4096,256]{1,0:T(8,128)(2,1)}), bf16[4096,256]{1,0:T(8,128)(2,1)}) %all-reduce.3.cloned.1.call-update) | async-done | bytes 2097168 | tf_op jit(solution)/shard_map/psum | solution.py:39
  392.4 0.0 copy-done.1
  392.4 1.6 convolution_convert_fusion
  394.0 0.0 all-gather.5.cloned.1.call-update
  394.1 0.0 all-reduce.5.cloned.1.call-start
  394.1 35.5 %all-gather.5.cloned.1.call-done = bf16[2048,256]{1,0:T(8,128)(2,1)} async-done(((bf16[128,256]{1,0:T(8,128)(2,1)}), bf16[2048,256]{1,0:T(8,128)(2,1)}) %all-gather.5.cloned.1.call-update) | async-done | bytes 1048592 | tf_op jit(solution)/shard_map/all_gather | solution.py:8
  429.6 1.9 gather_fusion.1
  431.5 2.4 multiply_bitcast_fusion
  433.9 3.6 copy.13
  437.4 2.4 broadcast.95
  439.9 9.5 %scatter_fusion.1 = f32[32,128,256]{2,1,0:T(8,128)} fusion(f32[32,128,256]{2,1,0:T(8,128)} %broadcast.95, s32[24]{0:T(128)S(1)} %bitcast.38, f32[24,128,256]{2,1,0:T(8,128)} %copy.13), kind=kCustom, calls=%fused_computation.3 | custom fusion | flops 786432 | bytes 9437280 | tf_op jit(solution)/shard_map/scatter-add | solution.py:36
  449.3 3.8 convert_element_type.48
  453.1 0.0 all-reduce.5.cloned.1.call-update
  453.2 315.8 %all-reduce.5.cloned.1.call-done = bf16[4096,256]{1,0:T(8,128)(2,1)} async-done(((bf16[4096,256]{1,0:T(8,128)(2,1)}), bf16[4096,256]{1,0:T(8,128)(2,1)}) %all-reduce.5.cloned.1.call-update) | async-done | bytes 2097168 | tf_op jit(solution)/shard_map/psum | solution.py:39
  769.0 1.5 convert_convert_fusion
  (2 shorter events, 0.0 us)
Async XLA Ops:
  6.5 48.5 %copy-start = (bf16[1,1,24,128,128]{4,3,2,1,0:T(8,128)(2,1)S(1)}, bf16[1,1,24,128,128]{4,3,2,1,0:T(8,128)(2,1)}, u32[]{:S(2)}) copy-start(bf16[1,1,24,128,128]{4,3,2,1,0:T(8,128)(2,1)} %param.10) | copy-start | bytes 2359300
  6.5 46.6 %all-gather.3.cloned.1.call-start = ((), (), s32[]{:S(2)}) async-start(), calls=%async_computation | async-start | bytes 1114112 | tf_op jit(solution)/shard_map/all_gather | solution.py:8
  8.4 384.0 %all-reduce.3.cloned.1.call-start = ((), (), s32[]{:S(2)}) async-start(), calls=%async_computation.1 | async-start | bytes 4194304 | tf_op jit(solution)/shard_map/psum | solution.py:39
  60.9 2.4 copy-start.2
  72.9 319.5 %copy-start.1 = (bf16[256,256]{1,0:T(8,128)(2,1)S(1)}, bf16[256,256]{1,0:T(8,128)(2,1)}, u32[]{:S(2)}) copy-start(bf16[256,256]{1,0:T(8,128)(2,1)} %param.9) | copy-start | bytes 393220
  76.7 352.9 %all-gather.5.cloned.1.call-start = ((), (), s32[]{:S(2)}) async-start(), calls=%async_computation.2 | async-start | bytes 1114112 | tf_op jit(solution)/shard_map/all_gather | solution.py:8
  394.1 374.9 %all-reduce.5.cloned.1.call-start = ((), (), s32[]{:S(2)}) async-start(), calls=%async_computation.3 | async-start | bytes 4194304 | tf_op jit(solution)/shard_map/psum | solution.py:39
Sparse Core Ops, SparseCore 0:
  9.5 43.5 all-gather.2
  76.8 315.4 all-reduce.2
  394.8 34.7 all-gather.4
  453.3 315.6 all-reduce.4
where the time goes:
time: 777 us
  waiting for transfers between devices  710 us (91%)
  other arithmetic  28.8 us (4%)
  local copies, waits for them, and re-layouts  15.7 us (2%)
  between operations  13.8 us (2%)
  matrix products  8.21 us (1%)
    psum x2, waiting for transfers between devices, body(): lax.psum(partial_value.astype(jnp.bfloat16), 'rep').astype(jnp.float32)  631 us
    all_gather x2, waiting for transfers between devices, tile_products(): gathered = lax.all_gather(panel_rows, 'blk', axis=0, tiled=True)  78.9 us
    scatter-add x2, other arithmetic, body(): jax.ops.segment_sum(masked, tile_row, num_segments=group_blocks)  19 us
  transfers between devices with their start and end apart: 4, of which 4 were waited for; matrix products, arithmetic and copies ran while one was open for 0% of the time, Pallas kernels for 0%

commit v1 on v0

v1 whole, which is shorter than its diff:
```python
import functools

import jax
import jax.numpy as jnp
from jax import lax
from jax.experimental import pallas as pl
from jax.experimental.pallas import tpu as pltpu
from jax.sharding import PartitionSpec as P

MESH = pl.DeviceIdType.MESH
NX, NY, NC = 4, 2, 2
NZ, NH = 16, 2
NB = NX * NY * NC
B, F, FH, CAP, GB = 128, 256, 128, 24, 32
HALF = NZ // 2
PIECES = 4
SLOTS = HALF + 1
PEERS = [(0, 1), (1, 0), (3, 0), (1, 1), (3, 1), (2, 0), (2, 1)]
BF, F32 = jnp.bfloat16, jnp.float32


def kernel(
    feat_hbm, w1_hbm, w2_hbm, tiles_hbm, rows_hbm, cols_hbm, count_hbm, out_ref,
    feat, w1, w2, tiles, rows, cols, count, rowm, prev, last,
    g00, g01, g10, g11, s0, s1, rbuf, own, hid, ysend, yrecv,
    in_sem, gsend, grecv, csend, crecv, ysend_sem, yrecv_sem,
):
    b, r = lax.axis_index("blk"), lax.axis_index("rep")
    core, ylo, x = lax.rem(b, NC), lax.rem(lax.div(b, NC), NY), lax.div(b, NC * NY)
    yhi, z = lax.rem(r, NH), lax.div(r, NH)

    def blk_at(dx, dy, dc):
        return (lax.rem(x + dx, NX) * NY + lax.rem(ylo + dy, NY)) * NC + lax.rem(core + dc, NC)

    up, down = lax.rem(z + 1, NZ) * NH + yhi, lax.rem(z + NZ - 1, NZ) * NH + yhi
    z_peer = (up, down)
    y_peer = z * NH + 1 - yhi
    sibling = blk_at(0, 0, 1)

    loads = [
        pltpu.make_async_copy(src, dst, in_sem.at[i])
        for i, (src, dst) in enumerate((
            (feat_hbm, feat), (w1_hbm, w1), (rows_hbm, rows), (cols_hbm, cols),
            (count_hbm, count), (tiles_hbm, tiles), (w2_hbm, w2),
        ))
    ]
    for load in loads:
        load.start()

    barrier = pltpu.get_barrier_semaphore()
    for dx, dy in PEERS:
        pl.semaphore_signal(barrier, inc=1, device_id=(blk_at(dx, dy, 0), r), device_id_type=MESH)
    pl.semaphore_signal(barrier, inc=1, device_id=(sibling, r), device_id_type=MESH)
    for peer in (up, down, y_peer):
        pl.semaphore_signal(barrier, inc=1, device_id=(b, peer), device_id_type=MESH)

    gath = ((g00, g01), (g10, g11))
    sums = (s0, s1)
    for s_ref in sums:
        s_ref[0] = jnp.zeros((B, FH), F32)

    def landed(ref, sem):
        pltpu.make_async_copy(ref, ref, sem).wait()

    def gather_copy(layer, half, slot, to):
        g = gath[layer][half]
        return pltpu.make_async_remote_copy(
            src_ref=g.at[slot], dst_ref=g.at[slot], send_sem=gsend.at[layer, half],
            recv_sem=grecv.at[layer, half, slot], device_id=(to, r), device_id_type=MESH,
        )

    def gather_start(layer, half):
        for dx, dy in PEERS:
            gather_copy(layer, half, b, blk_at(dx, dy, 0)).start()
        gather_copy(layer, half, b, sibling).start()

    def gather_finish(layer, half):
        g = gath[layer][half]
        for dx, dy in PEERS:
            source = blk_at(NX - dx, dy, 0)
            landed(g.at[source], grecv.at[layer, half, source])
            gather_copy(layer, half, source, sibling).start()
        for dx, dy in [(0, 0), *PEERS]:
            source = blk_at(NX - dx, dy, 1)
            landed(g.at[source], grecv.at[layer, half, source])

    def meta():
        for load in loads[2:5]:
            load.wait()
        live = count[0, 0]
        for k in range(CAP):
            rowm[k] = jnp.where(k < live, rows[0, 0, k], -1)

        def prev_of(k, carry):
            mine, found = rowm[k], jnp.int32(0)
            for j in range(CAP - 1):
                found = jnp.where((rowm[j] == mine) & (j < k), j + 1, found)
            prev[k] = found
            return carry

        lax.fori_loop(0, CAP, prev_of, 0)

        def last_of(g, carry):
            found = jnp.int32(0)
            for j in range(CAP):
                found = jnp.where(rowm[j] == g, j + 1, found)
            last[g] = found
            return carry

        lax.fori_loop(0, GB, last_of, 0)

    def products(layer, half):
        g, s_ref = gath[layer][half], sums[half]
        for k in range(CAP):
            block = g[cols[0, 0, k] // GB]
            s_ref[k + 1] = jnp.dot(tiles[0, 0, k], block, preferred_element_type=F32)

        def add(k, carry):
            s_ref[k + 1] = s_ref[k + 1] + s_ref[prev[k]]
            return carry

        lax.fori_loop(0, CAP, add, 0)

    def partial_of(target, piece):
        y = 1 - yhi if piece % 2 == 0 else yhi
        return sums[piece // 2][last[target * NH + y]]

    def target_at(d, step):
        return lax.rem(z + (HALF - step if d == 0 else HALF + step), NZ)

    def send_piece(layer, d, step, piece):
        pltpu.make_async_remote_copy(
            src_ref=rbuf.at[layer, d * SLOTS + step, piece],
            dst_ref=rbuf.at[layer, d * SLOTS + step + 1, piece],
            send_sem=csend.at[layer],
            recv_sem=crecv.at[layer, d * SLOTS + step + 1, piece],
            device_id=(b, z_peer[d]), device_id_type=MESH,
        ).start()

    def first_sends(layer, half):
        for step in range(2):
            for piece in (2 * half, 2 * half + 1):
                d = (piece + step) % 2
                rbuf[layer, d * SLOTS + step, piece] = partial_of(target_at(d, step), piece).astype(BF)
                send_piece(layer, d, step, piece)

    def chain_piece(layer, d, step, piece):
        slot = d * SLOTS + step
        landed(rbuf.at[layer, slot, piece], crecv.at[layer, slot, piece])
        total = rbuf[layer, slot, piece].astype(F32) + partial_of(target_at(d, step), piece)
        rbuf[layer, slot, piece] = total.astype(BF)
        send_piece(layer, d, step, piece)

    def y_copy(layer, half):
        return pltpu.make_async_remote_copy(
            src_ref=ysend.at[layer, half], dst_ref=yrecv.at[layer, half],
            send_sem=ysend_sem.at[layer, half], recv_sem=yrecv_sem.at[layer, half],
            device_id=(b, y_peer), device_id_type=MESH,
        )

    def reduce_scatter(layer):
        for piece in range(PIECES):
            chain_piece(layer, piece % 2, 1, piece)

        def step_body(step, carry):
            for piece in range(PIECES):
                for d in range(2):
                    chain_piece(layer, d, step, piece)
            return carry

        lax.fori_loop(2, HALF, step_body, 0)
        for piece in range(PIECES):
            total = partial_of(z, piece)
            for d in range(2):
                slot = d * SLOTS + HALF
                landed(rbuf.at[layer, slot, piece], crecv.at[layer, slot, piece])
                total += rbuf[layer, slot, piece].astype(F32)
            half = piece // 2
            if piece % 2 == 0:
                ysend[layer, half] = total.astype(BF)
                y_copy(layer, half).start()
            else:
                own[half] = total
        for half in range(2):
            y_copy(layer, half).wait_recv()
            total = own[half] + yrecv[layer, half].astype(F32)
            columns = pl.ds(half * FH, FH)
            if layer == 0:
                hid[:, columns] = jnp.maximum(total, 0.0).astype(BF)
            else:
                out_ref[:, columns] = total.astype(BF)

    for layer in range(2):
        if layer == 0:
            loads[0].wait()
            loads[1].wait()
        else:
            loads[6].wait()
        panel = jnp.dot(
            (feat, hid)[layer][...], (w1, w2)[layer][...], preferred_element_type=F32
        ).astype(BF)
        for half in range(2):
            gath[layer][half][b] = panel[:, half * FH : (half + 1) * FH]
        if layer == 0:
            pl.semaphore_wait(barrier, len(PEERS) + 4)
        for half in range(2):
            gather_start(layer, half)
        if layer == 0:
            meta()
            loads[5].wait()
        for half in range(2):
            gather_finish(layer, half)
            products(layer, half)
            first_sends(layer, half)
        reduce_scatter(layer)

    for layer in range(2):
        for half in range(2):
            landed(gath[layer][half].at[pl.ds(0, NB - 1)], gsend.at[layer, half])
            y_copy(layer, half).wait_send()
        landed(rbuf.at[layer, pl.ds(0, NZ - 1)], csend.at[layer])


def body(*args):
    vmem = pltpu.VMEM
    dma = pltpu.SemaphoreType.DMA
    return pl.pallas_call(
        kernel,
        out_shape=jax.ShapeDtypeStruct((B, F), BF),
        in_specs=[pl.BlockSpec(memory_space=pl.ANY)] * 7,
        out_specs=pl.BlockSpec(memory_space=pltpu.VMEM),
        scratch_shapes=[
            vmem((B, F), BF), vmem((F, F), BF), vmem((F, F), BF), vmem((1, 1, CAP, B, B), BF),
            pltpu.SMEM((1, 1, CAP), jnp.int32), pltpu.SMEM((1, 1, CAP), jnp.int32), pltpu.SMEM((1, 1), jnp.int32),
            pltpu.SMEM((CAP,), jnp.int32), pltpu.SMEM((CAP,), jnp.int32), pltpu.SMEM((GB,), jnp.int32),
            *[vmem((NB, B, FH), BF)] * 4,
            *[vmem((CAP + 1, B, FH), F32)] * 2,
            vmem((2, 2 * SLOTS, PIECES, B, FH), BF),
            vmem((2, B, FH), F32), vmem((B, F), BF),
            vmem((2, 2, B, FH), BF), vmem((2, 2, B, FH), BF),
            dma((7,)), dma((2, 2)), dma((2, 2, NB)),
            dma((2,)), dma((2, 2 * SLOTS, PIECES)), dma((2, 2)), dma((2, 2)),
        ],
        compiler_params=pltpu.CompilerParams(
            collective_id=0, has_side_effects=True, vmem_limit_bytes=40 * 2**20
        ),
        cost_estimate=pl.CostEstimate(
            flops=2 * CAP * 2 * B * B * F + 4 * B * F * F, bytes_accessed=2**21, transcendentals=0
        ),
    )(*args)


def solution(mesh):
    in_specs = (
        P(("blk", "rep"), None),
        P(),
        P(),
        P("blk", "rep", None, None, None),
        P("blk", "rep", None),
        P("blk", "rep", None),
        P("blk", "rep"),
    )
    out_specs = P(("blk", "rep"), None)
    return jax.shard_map(body, mesh=mesh, in_specs=in_specs, out_specs=out_specs, check_vma=False)
```

time: 777 us -> 102 us (0.13)
  the two profiles are of different devices: /device:TPU:6 before, /device:TPU:2 now
where the time goes in v1:
time: 102 us
  Pallas kernels  96.6 us (95%)
  local copies, waits for them, and re-layouts  4.41 us (4%)
    pallas_call x1, Pallas kernels, body(): pl.pallas_call(kernel, out_shape=jax.ShapeDtypeStruct((B, F), BF), in_spe...  96.6 us
    unnamed x13, local copies, waits for them, and re-layouts  4.41 us

profile of v1, /device:TPU:2, one launch (start us, length us, event | category | flops | bytes accessed | tf_op | source)
XLA Modules:
  0.0 101.8 jit_solution(7409851080175497095)
XLA Ops:
  0.0 0.0 copy-start.5
  0.0 0.0 copy-start.4
  0.7 0.0 copy-done.5
  0.7 0.0 copy-done.4
  0.7 0.0 copy-start
  0.7 1.1 %copy-done = bf16[1,1,24,128,128]{4,3,2,1,0:T(8,128)(2,1)S(1)} copy-done((bf16[1,1,24,128,128]{4,3,2,1,0:T(8,128)(2,1)S(1)}, bf16[1,1,24,128,128]{4,3,2,1,0:T(8,128)(2,1)}, u32[]{:S(2)}) %copy-start) | copy-done | bytes 786456
  1.8 0.0 copy-start.1
  1.8 0.9 copy-done.1
  2.7 0.0 copy-start.2
  2.7 0.9 copy-done.2
  3.6 0.0 copy-start.3
  3.6 0.8 copy-done.3
  4.5 96.6 %shard_map.73 = bf16[128,256]{1,0:T(8,128)(2,1)S(1)} custom-call(bf16[128,256]{1,0:T(8,128)(2,1)S(1)} %copy-done.3, bf16[256,256]{1,0:T(8,128)(2,1)S(1)} %copy-done.1, bf16[256,256]{1,0:T(8,128)(2,1)S(1)} %copy-done.2, bf16[1,1,24,128,128]{4,3,2,1,0:T(8,128)(2,1)S(1)} %copy-done, s32[1,1,24]{2,1,0:T(1,128)S(1)} %copy-done.4, s32[1,1,24]{2,1,0:T(1,128)S(1)} %copy-done.5, ...), custom_call_target="tpu_custom_call" | custom-call | flops 436207616 | bytes 2097152 | tf_op jit(solution)/shard_map/pallas_call | solution.py:227
  101.1 0.6 copy.10
Async XLA Ops:
  0.0 0.7 copy-start.5
  0.0 0.7 copy-start.4
  0.7 1.1 %copy-start = (bf16[1,1,24,128,128]{4,3,2,1,0:T(8,128)(2,1)S(1)}, bf16[1,1,24,128,128]{4,3,2,1,0:T(8,128)(2,1)}, u32[]{:S(2)}) copy-start(bf16[1,1,24,128,128]{4,3,2,1,0:T(8,128)(2,1)} %tiles_hbm.1) | copy-start | bytes 2359300
  1.8 0.9 copy-start.1
  2.7 0.9 copy-start.2
  3.6 0.8 copy-start.3
